TPU v7x, 32 devices: a whole 2x2x4 slice. The times are simulated.
32 devices in a mesh: seq: 8 (over z, x), rep: 4 (over y, core).
Axes of the slice: x: 2, y: 2, z: 4, core: 2. Of those that a mesh axis runs over, the one named last changes fastest.
Arguments:
- tokens: bfloat16 [4096, 2304], P(('rep', 'seq')), parts along dimension 0, may hold values from -6 to 6
- qkv_weight: bfloat16 [2304, 6144], P(None, 'seq'), may hold values from -0.125 to 0.125
- conv_weight: float32 [4, 6144], replicated, may hold values from -3 to 3
- decay_down: bfloat16 [2304, 128], replicated, may hold values from -0.125 to 0.125
- decay_up: bfloat16 [128, 2048], replicated, may hold values from -0.5 to 0.5
- decay_rate: float32 [2048], replicated, may hold values from 0.0009765625 to 0.1
- beta_weight: bfloat16 [2304, 16], replicated, may hold values from -0.125 to 0.125
- beta_scale: float32 [16], replicated, may hold values from 0.125 to 1
- gate_down: bfloat16 [2304, 128], replicated, may hold values from -0.125 to 0.125
- gate_up: bfloat16 [128, 2048], replicated, may hold values from -0.5 to 0.5
- norm_gain: float32 [128], replicated, may hold values from 0.1 to 1.9
Outputs:
- attended: bfloat16 [4096, 2048], P(('rep', 'seq')), parts along dimension 0
There are 4 independent parts, one for each index of `rep`. A program takes and returns all parts, laid end to end along the dimension named above; an argument that names none is the same for every part. Nothing has to cross between parts.
All inputs are finite; a program needn't handle non-finite values.
Results may differ from a plain program's by a relative error of at most 0.0054.
Values may be sent and summed in bfloat16 or wider, within the bound.
A program may use at most 192 MiB of HBM per device.

v0:
```python
import jax
import jax.numpy as jnp
from jax import lax
from jax.sharding import PartitionSpec as P

H = 16
DK = 128
CONV = 4
BLOCK = 64


precise = lax.Precision.HIGHEST


def from_behind(block, axis, distance):
    devices = range(lax.axis_size(axis))
    route = [(i - distance, i) for i in devices if i - distance in devices]
    return lax.ppermute(block, axis, route)


def carried_in(x, axis, combine, identity):
    devices, mine = (lax.axis_size(axis), lax.axis_index(axis))
    everything = jax.tree.map(lambda part: lax.all_gather(part, axis), x)
    start = jax.tree.map(
        lambda part, zero: jnp.broadcast_to(jnp.asarray(zero, part.dtype), part.shape), x, identity
    )

    def lap(k, before):
        reached = k < mine
        new = combine(before, jax.tree.map(lambda part: part[k], everything))
        return jax.tree.map(lambda a, b: jnp.where(reached, a, b), new, before)

    return lax.fori_loop(0, devices, lap, start)


def unit_rows(vector):
    return vector * lax.rsqrt(jnp.sum(vector * vector, axis=-1, keepdims=True) + 1e-06)


def features(padded, count, conv_weight):
    combined = conv_weight[0] * padded[0:count].astype(jnp.float32)
    for offset in range(1, CONV):
        combined = combined + conv_weight[offset] * padded[offset : offset + count].astype(
            jnp.float32
        )
    active = jax.nn.silu(combined).reshape(count, 3, H, DK)
    query = unit_rows(active[:, 0]) * DK ** (-0.5)
    keys = unit_rows(active[:, 1])
    values = active[:, 2]
    return (query, keys, values)


def gates(tokens, decay_down, decay_up, decay_rate, beta_weight, beta_scale, gate_down, gate_up):
    beta = beta_scale * jax.nn.sigmoid(
        jnp.dot(tokens, beta_weight, preferred_element_type=jnp.float32)
    )
    decay_low = jnp.dot(tokens, decay_down, preferred_element_type=jnp.float32).astype(jnp.bfloat16)
    logdec = -decay_rate * jax.nn.sigmoid(
        jnp.dot(decay_low, decay_up, preferred_element_type=jnp.float32)
    )
    gate_low = jnp.dot(tokens, gate_down, preferred_element_type=jnp.float32).astype(jnp.bfloat16)
    gate_value = jax.nn.sigmoid(jnp.dot(gate_low, gate_up, preferred_element_type=jnp.float32))
    return (beta, logdec, gate_value)


def to_blocks(array, count):
    return array.reshape(count // BLOCK, BLOCK, H, array.shape[-1]).transpose(0, 2, 1, 3)


def block_terms(query, keys, values, beta, logdec):
    log_sum = jnp.cumsum(logdec, axis=2)
    grow = jnp.exp(log_sum)
    keys_up = keys * grow
    keys_down = keys * jnp.exp(-log_sum)
    query_up = query * grow
    keys_end = keys * jnp.exp(log_sum[:, :, -1:, :] - log_sum)
    length = query.shape[2]
    rows = lax.broadcasted_iota(jnp.int32, (length, length), 0)
    columns = lax.broadcasted_iota(jnp.int32, (length, length), 1)
    scores = jnp.einsum("nhic,nhjc->nhij", keys_up, keys_down, precision=precise) * beta[..., None]
    system = jnp.where(rows > columns, scores, 0.0) + jnp.eye(length, dtype=jnp.float32)
    right_side = jnp.concatenate([values, keys_up], axis=-1) * beta[..., None]
    solved = jax.scipy.linalg.solve_triangular(system, right_side, lower=True, unit_diagonal=True)
    values_w = solved[..., :DK]
    keys_w = solved[..., DK:]
    attend = jnp.where(
        rows >= columns, jnp.einsum("nhic,nhjc->nhij", query_up, keys_down, precision=precise), 0.0
    )
    decay_end = jnp.exp(log_sum[:, :, -1, :])
    return (query_up, keys_end, values_w, keys_w, attend, decay_end)


def advance(state, inputs):
    query_up, keys_end, values_w, keys_w, attend, decay_end = inputs
    update = values_w - jnp.einsum("hcd,hde->hce", keys_w, state, precision=precise)
    output = jnp.einsum("hcd,hde->hce", query_up, state, precision=precise)
    output = output + jnp.einsum("hij,hje->hie", attend, update, precision=precise)
    state = decay_end[..., None] * state + jnp.einsum(
        "hcd,hce->hde", keys_end, update, precision=precise
    )
    return (state, output)


def matmul(left, right):
    return jnp.einsum("...de,...ef->...df", left, right, precision=precise)


def fold_block(carry, inputs):
    matrix, offset = carry
    keys_end, keys_w, values_w, decay_end = inputs
    eye_block = jnp.eye(DK, dtype=jnp.float32)
    block_matrix = decay_end[..., None] * eye_block - jnp.einsum(
        "hcd,hce->hde", keys_end, keys_w, precision=precise
    )
    block_offset = jnp.einsum("hcd,hce->hde", keys_end, values_w, precision=precise)
    return ((matmul(block_matrix, matrix), matmul(block_matrix, offset) + block_offset), None)


def join_pairs(first, second):
    return (matmul(second[0], first[0]), matmul(second[0], first[1]) + second[1])


def finish(core, gate_value, norm_gain, count):
    scaled = core * lax.rsqrt(jnp.mean(core * core, axis=-1, keepdims=True) + 1e-06) * norm_gain
    return (scaled.reshape(count, H * DK) * gate_value).astype(jnp.bfloat16)


def per_device(
    tokens,
    qkv_weight,
    conv_weight,
    decay_down,
    decay_up,
    decay_rate,
    beta_weight,
    beta_scale,
    gate_down,
    gate_up,
    norm_gain,
):
    count = tokens.shape[0]
    mixed = jnp.dot(
        tokens,
        lax.all_gather(qkv_weight, "seq", axis=1, tiled=True),
        preferred_element_type=jnp.float32,
    ).astype(jnp.bfloat16)
    earlier = from_behind(mixed[count - (CONV - 1) :], "seq", 1)
    padded = jnp.concatenate([earlier, mixed], axis=0)
    query, keys, values = features(padded, count, conv_weight)
    beta, logdec, gate_value = gates(
        tokens, decay_down, decay_up, decay_rate, beta_weight, beta_scale, gate_down, gate_up
    )
    beta_blocks = beta.reshape(count // BLOCK, BLOCK, H).transpose(0, 2, 1)
    terms = block_terms(
        to_blocks(query, count),
        to_blocks(keys, count),
        to_blocks(values, count),
        beta_blocks,
        to_blocks(logdec.reshape(count, H, DK), count),
    )
    query_up, keys_end, values_w, keys_w, attend, decay_end = terms
    identity = jnp.broadcast_to(jnp.eye(DK, dtype=jnp.float32), (H, DK, DK))
    zeroed = jnp.zeros((H, DK, DK), jnp.float32)
    (matrix, offset), unused = lax.scan(
        fold_block, (identity, zeroed), (keys_end, keys_w, values_w, decay_end)
    )

    def combine(earlier_pair, later_pair):
        return join_pairs(earlier_pair, later_pair)

    prefix = carried_in((matrix, offset), "seq", combine, (identity, zeroed))
    incoming = prefix[1]
    final_state, outputs = lax.scan(advance, incoming, terms)
    core = outputs.transpose(0, 2, 1, 3).reshape(count, H, DK)
    return finish(core, gate_value, norm_gain, count)


def solution(mesh):
    in_specs = (
        P(("rep", "seq"), None),
        P(None, "seq"),
        P(),
        P(),
        P(),
        P(),
        P(),
        P(),
        P(),
        P(),
        P(),
    )
    out_specs = P(("rep", "seq"), None)
    return jax.shard_map(
        per_device, mesh=mesh, in_specs=in_specs, out_specs=out_specs, check_vma=False
    )
```

profile of v0, /device:TPU:0, one launch (start us, length us, event | category | flops | bytes accessed | tf_op | source)
XLA Modules:
  0.0 1065.8 jit_solution(3468585397718762380)
XLA Ops:
  9.0 13.1 %fusion.63 = f32[2,16,64,128]{3,1,2,0:T(8,128)S(1)} fusion(f32[2,64,16,128]{3,2,1,0:T(8,128)S(1)} %bitcast.180), kind=kOutput, calls=%fused_computation.87 | output fusion | flops 16515072 | bytes 2097152 | tf_op jit(solution)/shard_map/jit(cumsum)/reduce_window_sum | solution.py:71
  23.5 527.5 %all-gather.6.cloned.1.call-done = bf16[2304,6144]{1,0:T(8,128)(2,1)} async-done(((bf16[2304,768]{1,0:T(8,128)(2,1)}), bf16[2304,6144]{1,0:T(8,128)(2,1)}) %all-gather.6.cloned.1.call-update) | async-done | bytes 28311568 | tf_op jit(solution)/shard_map/all_gather | solution.py:144
  551.1 12.9 %convolution_convert_fusion = bf16[128,6144]{1,0:T(8,128)(2,1)S(1)} fusion(bf16[128,2304]{1,0:T(8,128)(2,1)S(1)} %copy-done, bf16[2304,6144]{1,0:T(8,128)(2,1)} %all-gather.6.cloned.1.call-done), kind=kOutput, calls=%fused_computation.48 | convolution fusion | flops 3624665088 | bytes 30474240 | tf_op jit(solution)/shard_map/dot_general | solution.py:142
  574.9 3.3 fusion.57
  578.2 158.7 %custom-call.4 = f32[2,16,1,64,64]{3,4,2,1,0:T(8,128)} custom-call(f32[2,16,1,64,64]{4,3,2,1,0:T(8,128)} %fusion.57), custom_call_target="InvertDiagBlocksLowerTriangular" | custom-call | tf_op jit(solution)/shard_map/jit(_solve_triangular)/vmap(vmap())/triangular_solve | solution.py:83
  738.5 3.0 fusion.48
  743.2 17.4 %while.40 = (s32[]{:T(128)}, f32[16,128,128]{2,1,0:T(8,128)S(1)}, f32[16,128,128]{2,1,0:T(8,128)}, f32[2,16,128]{2,1,0:T(8,128)S(1)}, f32[2,16,64,128]{3,2,1,0:T...) while((s32[]{:T(128)}, f32[16,128,128]{2,1,0:T(8,128)S(1)}, ...), condition=%wide.region_3.4_spmd.clone, body=%wide.region_2.3_spmd.clone.sunk | while | flops 1209040896 | bytes 22177964 | solution.py:164
  743.6 3.2 convolution_subtract_fusion.5
  748.0 2.9 convolution_add_fusion.7
  752.2 3.2 convolution_subtract_fusion.5
  756.6 2.9 convolution_add_fusion.7
  764.3 4.8 convolution_select_fusion
  769.1 119.5 %all-gather.10.cloned.1.call-done = f32[128,128,128]{2,1,0:T(8,128)} async-done(((f32[16,128,128]{2,1,0:T(8,128)}), f32[128,128,128]{2,1,0:T(8,128)}) %all-gather.10.cloned.1.call-update) | async-done | bytes 8388624 | tf_op jit(solution)/shard_map/all_gather | solution.py:23
  888.6 125.3 %all-gather.8.cloned.1.call-done = f32[128,128,128]{2,1,0:T(8,128)} async-done(((f32[16,128,128]{2,1,0:T(8,128)}), f32[128,128,128]{2,1,0:T(8,128)}) %all-gather.8.cloned.1.call-update) | async-done | bytes 8388624 | tf_op jit(solution)/shard_map/all_gather | solution.py:23
  1013.9 23.5 %while.41 = (s32[]{:T(128)}, f32[16,128,128]{2,1,0:T(8,128)S(1)}, s32[]{:T(128)}, f32[8,16,128,128]{3,2,1,0:T(8,128)}, f32[8,16,128,128]{3,2,1,0:T(8,128)}, /*index=5*/s32[]{:T(128)}, s32[]{:T(128)}) while((s32[]{:T(128)}, f32[16,128,128]{2,1,0:T(8,128)S(1)}, s32[]{:T(128)}, f32[8,16,128,128]{3,2,1,0:T(8,128)}, ...), condition=%wide.region_5.6_spmd.clone, body=%wide.region_4.5_spmd.clone.sunk | while | flops 403701760 | bytes 7342695 | solution.py:33
  1014.0 2.8 fusion.141
  1016.9 2.8 fusion.141
  1019.8 2.8 fusion.141
  1022.8 2.8 fusion.141
  1025.7 2.8 fusion.141
  1028.7 2.8 fusion.141
  1034.5 2.8 fusion.141
  1037.4 15.1 %while.39 = (s32[]{:T(128)}, f32[16,128,128]{2,1,0:T(8,128)S(1)}, f32[2,16,64,128]{3,2,1,0:T(8,128)}, f32[2,16,128]{2,1,0:T(8,128)S(1)}, f32[2,16,64,128]{3,2,1,...) while((s32[]{:T(128)}, f32[16,128,128]{2,1,0:T(8,128)S(1)}, ...), condition=%wide.region_8.9_spmd, body=%wide.region_7.8_spmd.sunk | while | flops 705429504 | bytes 22571212 | solution.py:173
  1056.3 2.9 fusion.47
  (120 shorter events, 48.5 us)
Async XLA Ops:
  6.5 1.1 copy-start
  6.5 1.3 copy-start.18
  6.5 1.4 copy-start.16
  6.5 544.5 %all-gather.6.cloned.1.call-start = ((), (), s32[]{:S(2)}) async-start(), calls=%async_computation | async-start | bytes 31850496 | tf_op jit(solution)/shard_map/all_gather | solution.py:144
  7.3 881.3 %all-gather.10.cloned.1.call-start = ((), (), s32[]{:S(2)}) async-start(), calls=%async_computation.2 | async-start | bytes 9437184 | tf_op jit(solution)/shard_map/all_gather | solution.py:23
  8.7 14.5 %copy-start.12 = (bf16[2304,16]{0,1:T(8,128)(2,1)S(1)}, bf16[2304,16]{0,1:T(8,128)(2,1)}, u32[]{:S(2)}) copy-start(bf16[2304,16]{0,1:T(8,128)(2,1)} %param.23) | copy-start | bytes 221188
  8.7 14.5 %copy-start.14 = (f32[16]{0:T(128)S(1)}, f32[16]{0:T(128)}, u32[]{:S(2)}) copy-start(f32[16]{0:T(128)} %param.24) | copy-start | bytes 196
  8.7 14.8 %copy-start.11 = (f32[4,6144]{1,0:T(4,128)S(1)}, f32[4,6144]{1,0:T(4,128)}, u32[]{:S(2)}) copy-start(f32[4,6144]{1,0:T(4,128)} %param.19) | copy-start | bytes 294916
  564.0 4.0 collective-permute-start
  570.7 1.7 copy-start.7
  736.8 1.7 copy-start.10
  743.2 18.6 %copy-start.15 = (f32[128]{0:T(128)S(1)}, f32[128]{0:T(128)}, u32[]{:S(2)}) copy-start(f32[128]{0:T(128)} %param.27) | copy-start | bytes 1540
  743.5 3.3 copy-start.2
  743.6 4.4 copy-start.3
  752.0 3.3 copy-start.2
  752.2 4.4 copy-start.3
  760.7 253.2 %all-gather.8.cloned.1.call-start = ((), (), s32[]{:S(2)}) async-start(), calls=%async_computation.1 | async-start | bytes 9437184 | tf_op jit(solution)/shard_map/all_gather | solution.py:23
  1037.4 4.1 copy-start.4
  1037.4 4.1 copy-start.8
  1042.6 2.3 copy-start.9
  1044.9 4.1 copy-start.4
  1044.9 4.1 copy-start.8
  1050.1 2.3 copy-start.9
  1052.4 3.9 copy-start.17
  (4 other events, 3.8 us)
Sparse Core Ops, SparseCore 0:
  8.9 542.1 all-gather.5
  760.8 127.7 all-gather.9
  890.7 123.1 all-gather.7
where the time goes:
time: 1070 us
  waiting for transfers between devices  774 us (72%)
  other arithmetic  181 us (17%)
  matrix products  82 us (8%)
  between operations  13.5 us (1%)
  local copies, waits for them, and re-layouts  12 us (1%)
    all_gather x1, waiting for transfers between devices, per_device(): lax.all_gather(qkv_weight, 'seq', axis=1, tiled=True)  528 us
    all_gather x2, waiting for transfers between devices, carried_in(): everything = jax.tree.map(lambda part: lax.all_gather(part, axis), x)  245 us
    another operation x2, other arithmetic, block_terms(): jax.scipy.linalg.solve_triangular(system, right_side, lower=True, unit_di...  159 us
    dot_general x12, matrix products, matmul(): return jnp.einsum('...de,...ef->...df', left, right, precision=precise)  27.2 us
  transfers between devices with their start and end apart: 4, of which 4 were waited for; matrix products, arithmetic and copies ran while one was open for 2% of the time, Pallas kernels for 0%

commit v1 on v0

--- a/solution.py
+++ b/solution.py
@@ -1,6 +1,9 @@
+import functools
 import jax
 import jax.numpy as jnp
 from jax import lax
+from jax.experimental import pallas as pl
+from jax.experimental.pallas import tpu as pltpu
 from jax.sharding import PartitionSpec as P
 
 H = 16
@@ -125,7 +128,7 @@
     return (scaled.reshape(count, H * DK) * gate_value).astype(jnp.bfloat16)
 
 
-def per_device(
+def tokens_split(
     tokens,
     qkv_weight,
     conv_weight,
@@ -175,6 +178,218 @@
     return finish(core, gate_value, norm_gain, count)
 
 
+CHUNK = 128
+NN = (((1,), (0,)), ((), ()))
+NT = (((1,), (1,)), ((), ()))
+TN = (((0,), (0,)), ((), ()))
+
+
+def mm(a, b, dims=NN):
+    return lax.dot_general(a, b, dims, preferred_element_type=jnp.float32)
+
+
+def low(a):
+    return a.astype(jnp.bfloat16)
+
+
+def split(a):
+    top = low(a)
+    return top, low(a - top.astype(jnp.float32))
+
+
+def mm3(a, b, dims=NN):
+    (ah, al), (bh, bl) = a, b
+    return mm(ah, bh, dims) + (mm(ah, bl, dims) + mm(al, bh, dims))
+
+
+def product(level):
+    if level == 1:
+        return low, mm
+    return split, mm3
+
+
+LEVELS = {"g": 3, "t": 1, "s": 3, "m": 3, "c": 3}
+
+
+def sigmoid(u):
+    return 1.0 / (1.0 + jnp.exp(-u))
+
+
+def project(rows, tok, w_at, gate_refs, mixed_s, low_s, beta_s):
+    dd, gd, bw, bs = gate_refs
+    width = w_at(0).shape[1]
+    for t in range(3):
+        got = mm(tok, w_at(t)).astype(jnp.bfloat16).astype(jnp.float32)
+        mixed_s[pl.ds(pl.multiple_of(rows + 8, 8), tok.shape[0]), t * width : (t + 1) * width] = got
+    low_s[pl.ds(rows, tok.shape[0]), :DK] = low(mm(tok, dd[...]))
+    low_s[pl.ds(rows, tok.shape[0]), DK:] = low(mm(tok, gd[...]))
+    beta_s[pl.ds(rows, tok.shape[0]), :] = bs[...] * sigmoid(mm(tok, bw[...]))
+
+
+def chunk_terms(places, me, heads, refs, scratch, terms):
+    conv, du, rate = refs
+    mixed_s, low_s, beta_s = scratch
+    m_s, b_s, p_s, q_s = terms
+    C = CHUNK
+    width = heads * DK
+    rows = lax.broadcasted_iota(jnp.int32, (C, C), 0)
+    cols = lax.broadcasted_iota(jnp.int32, (C, C), 1)
+    tril = jnp.where(rows >= cols, 1.0, 0.0).astype(jnp.bfloat16)
+    eye = jnp.where(rows == cols, 1.0, 0.0)
+    total = conv.shape[1] // 3
+
+    def part(t, chunk, h):
+        at = pl.multiple_of(t * total + me * width + h * DK, DK)
+        acc = None
+        near = mixed_s[pl.ds(pl.multiple_of(chunk * C, C), C + 8), t * width + h * DK : t * width + (h + 1) * DK]
+        for j in range(CONV):
+            got = near[8 - (CONV - 1) + j : 8 - (CONV - 1) + j + C]
+            term = conv[j : j + 1, pl.ds(at, DK)] * got
+            acc = term if acc is None else acc + term
+        return acc * sigmoid(acc)
+
+    def unit(a):
+        return a * lax.rsqrt(jnp.sum(a * a, axis=-1, keepdims=True) + 1e-06)
+
+    stage = []
+    for chunk, h in places:
+        q = unit(part(0, chunk, h)) * DK ** (-0.5)
+        k = unit(part(1, chunk, h))
+        v = part(2, chunk, h)
+        at = pl.multiple_of(me * width + h * DK, DK)
+        down = low_s[pl.ds(pl.multiple_of(chunk * C, C), C), :DK]
+        logdec = -rate[:, pl.ds(at, DK)] * sigmoid(mm(down, du[:, pl.ds(at, DK)]))
+        every = beta_s[pl.ds(pl.multiple_of(chunk * C, C), C), :]
+        lane = lax.broadcasted_iota(jnp.int32, every.shape, 1)
+        beta = jnp.sum(jnp.where(lane == me * heads + h, every, 0.0), axis=1, keepdims=True)
+        lh, ll = split(logdec)
+        ls = mm(tril, lh) + mm(tril, ll)
+        last = ls[C - 1 : C, :]
+        grow = jnp.exp(ls)
+        kup = k * grow
+        stage.append((kup, k * jnp.exp(-ls), q * grow, k * jnp.exp(last - ls), v, beta, jnp.exp(last)))
+    cut, dot = product(LEVELS["g"])
+    lowers, attends = [], []
+    for kup, kdown, qup, kend, v, beta, dec in stage:
+        kd = cut(kdown)
+        lowers.append(jnp.where(rows > cols, dot(cut(kup), kd, NT) * beta, 0.0))
+        attends.append(jnp.where(rows >= cols, dot(cut(qup), kd, NT), 0.0))
+    cut, dot = product(LEVELS["t"])
+    inverse = [eye - jnp.where(rows // 2 == cols // 2, low_, 0.0) for low_ in lowers]
+    size = 2
+    while size < C:
+        mask = jnp.logical_and(rows // (2 * size) == cols // (2 * size), rows // size != cols // size)
+        ts = [cut(t) for t in inverse]
+        mid = [dot(cut(jnp.where(mask, low_, 0.0)), t) for low_, t in zip(lowers, ts)]
+        inverse = [t - dot(tc, cut(x)) for t, tc, x in zip(inverse, ts, mid)]
+        size *= 2
+    cut, dot = product(LEVELS["s"])
+    solved = []
+    for t, (kup, kdown, qup, kend, v, beta, dec) in zip(inverse, stage):
+        tc = cut(t)
+        solved.append((dot(tc, cut(v * beta)), dot(tc, cut(kup * beta))))
+    cut, dot = product(LEVELS["m"])
+    for (chunk, h), (vw, kw), at, (kup, kdown, qup, kend, v, beta, dec) in zip(places, solved, attends, stage):
+        vc, kc, ac, ec = cut(vw), cut(kw), cut(at), cut(kend)
+        slot = chunk * heads + h
+        p_s[slot] = dot(ac, vc)
+        q_s[slot] = qup - dot(ac, kc)
+        m_s[slot] = eye * dec - dot(ec, kc, TN)
+        b_s[slot] = dot(ec, vc, TN)
+
+
+def run_states(chunks, me, heads, refs, low_s, terms, states, put):
+    gu, gain = refs
+    m_s, b_s, p_s, q_s = terms
+    C = CHUNK
+    width = heads * DK
+    cut, dot = product(LEVELS["c"])
+    for h in range(heads):
+        states[h] = jnp.zeros((DK, DK), jnp.float32)
+
+    def step(chunk, carry):
+        for h in range(heads):
+            slot = chunk * heads + h
+            s = cut(states[h])
+            core = p_s[slot] + dot(cut(q_s[slot]), s)
+            states[h] = dot(cut(m_s[slot]), s) + b_s[slot]
+            at = pl.multiple_of(me * width + h * DK, DK)
+            gate = sigmoid(mm(low_s[pl.ds(pl.multiple_of(chunk * C, C), C), DK:], gu[:, pl.ds(at, DK)]))
+            core = core * lax.rsqrt(jnp.mean(core * core, axis=-1, keepdims=True) + 1e-06) * gain[...]
+            put(chunk, h, low(core * gate))
+        return carry
+
+    lax.fori_loop(0, chunks, step, 0)
+
+
+def heads_kernel(n, heads, tok, w, conv, dd, du, rate, bw, bs, gd, gu, gain, out, mixed_s, low_s, beta_s, m_s, b_s, p_s, q_s, states):
+    me = lax.axis_index("seq")
+    count = tok.shape[0]
+    chunks = count // CHUNK
+    mixed_s[0:8, :] = jnp.zeros((8, mixed_s.shape[1]), jnp.float32)
+
+    def w_at(t):
+        return w[lax.rem(t * n + me, 3)]
+
+    def first(c, carry):
+        rows = pl.multiple_of(c * CHUNK, CHUNK)
+        project(rows, tok[pl.ds(rows, CHUNK), :], w_at, (dd, gd, bw, bs), mixed_s, low_s, beta_s)
+        return carry
+
+    lax.fori_loop(0, chunks, first, 0)
+
+    def second(c, carry):
+        places = [(c * 2 + i, h) for i in range(2) for h in range(heads)]
+        chunk_terms(places, me, heads, (conv, du, rate), (mixed_s, low_s, beta_s), (m_s, b_s, p_s, q_s))
+        return carry
+
+    lax.fori_loop(0, chunks // 2, second, 0)
+
+    def put(chunk, h, value):
+        out[pl.ds(pl.multiple_of(chunk * CHUNK, CHUNK), CHUNK), h * DK : (h + 1) * DK] = value
+
+    run_states(chunks, me, heads, (gu, gain), low_s, (m_s, b_s, p_s, q_s), states, put)
+
+
+def heads_split(tokens, qkv_weight, conv_weight, decay_down, decay_up, decay_rate, beta_weight, beta_scale, gate_down, gate_up, norm_gain):
+    n, reps = lax.axis_size("seq"), lax.axis_size("rep")
+    rep = lax.axis_index("rep")
+    depth = qkv_weight.shape[0]
+    heads = H // n
+    width = heads * DK
+    share = depth // reps
+    everything = lax.all_gather(tokens, "seq", axis=0, tiled=True)
+    mine = lax.dynamic_slice_in_dim(qkv_weight, rep * share, share, 0)
+    pieces = [
+        lax.ppermute(mine[:, j * width : (j + 1) * width], "seq", [(s, (3 * s + j) % n) for s in range(n)])
+        for j in range(3)
+    ]
+    weight = lax.all_gather(jnp.stack(pieces), "rep", axis=1, tiled=True)
+    count = everything.shape[0]
+    slots = count // CHUNK * heads
+    square = pltpu.VMEM((slots, DK, DK), jnp.float32)
+    attended = pl.pallas_call(
+        functools.partial(heads_kernel, n, heads),
+        out_shape=jax.ShapeDtypeStruct((count, width), jnp.bfloat16),
+        in_specs=[pl.BlockSpec(memory_space=pltpu.VMEM)] * 11,
+        out_specs=pl.BlockSpec(memory_space=pltpu.VMEM),
+        scratch_shapes=[
+            pltpu.VMEM((count + 8, 3 * width), jnp.float32),
+            pltpu.VMEM((count, 2 * DK), jnp.bfloat16),
+            pltpu.VMEM((count, H), jnp.float32),
+            square, square, square, square,
+            pltpu.VMEM((heads, DK, DK), jnp.float32),
+        ],
+        compiler_params=pltpu.CompilerParams(vmem_limit_bytes=48 * 2**20),
+    )(everything, weight, conv_weight, decay_down, decay_up, decay_rate.reshape(1, -1), beta_weight, beta_scale.reshape(1, -1), gate_down, gate_up, norm_gain.reshape(1, -1))
+    return lax.all_to_all(attended, "seq", 0, 1, tiled=True)
+
+
+def by_heads(mesh):
+    n, reps = mesh.shape["seq"], mesh.shape["rep"]
+    return H % n == 0 and n % 3 != 0
+
+
 def solution(mesh):
     in_specs = (
         P(("rep", "seq"), None),
@@ -191,5 +406,5 @@
     )
     out_specs = P(("rep", "seq"), None)
     return jax.shard_map(
-        per_device, mesh=mesh, in_specs=in_specs, out_specs=out_specs, check_vma=False
-    )
+        heads_split if by_heads(mesh) else tokens_split, mesh=mesh, in_specs=in_specs, out_specs=out_specs, check_vma=False
+    )

time: 1070 us -> 204 us (0.19)
  waiting for transfers between devices: 774 us -> 128 us
  other arithmetic: 181 us -> 1.09 us
  matrix products: 82 us -> 0 us
  Pallas kernels: 0 us -> 30.6 us
  blocking collectives: 0 us -> 17.2 us
    all_gather x3 -> x2, waiting for transfers between devices: 772 us -> 121 us  [the longest x1 82.1 us: heads_split(): everything = lax.all_gather(tokens, 'seq', axis=0, tiled=True)]
    another operation x3 -> x1, other arithmetic: 172 us -> 1.09 us  [heads_split(): weight = lax.all_gather(jnp.stack(pieces), 'rep', axis=1, tiled=True)]
    dot_general x30 -> x0, matrix products: 79 us -> none  [the longest x12 27.2 us: matmul(): return jnp.einsum('...de,...ef->...df', left, right, precision=precise)]
    pallas_call x0 -> x1, Pallas kernels: none -> 30.6 us  [heads_split(): pl.pallas_call(functools.partial(heads_kernel, n, heads), out_shape=jax.S...]
    all_to_all x0 -> x1, blocking collectives: none -> 17.2 us  [heads_split(): return lax.all_to_all(attended, 'seq', 0, 1, tiled=True)]
  transfers between devices with their start and end apart: 4 -> 5, of which waited for: 4 -> 4; matrix products, arithmetic and copies ran while one was open for 2% -> 0% of each run, Pallas kernels for 0% -> 0%
where the time goes in v1:
time: 204 us
  waiting for transfers between devices  128 us (63%)
  Pallas kernels  30.6 us (15%)
  blocking collectives  17.2 us (8%)
  between operations  13.5 us (7%)
  starting transfers between devices  10.9 us (5%)
  local copies, waits for them, and re-layouts  2.57 us (1%)
    all_gather x1, waiting for transfers between devices, heads_split(): everything = lax.all_gather(tokens, 'seq', axis=0, tiled=True)  82.1 us
    all_gather x1, waiting for transfers between devices, heads_split(): weight = lax.all_gather(jnp.stack(pieces), 'rep', axis=1, tiled=True)  38.5 us
    pallas_call x1, Pallas kernels, heads_split(): pl.pallas_call(functools.partial(heads_kernel, n, heads), out_shape=jax.S...  30.6 us
    all_to_all x1, blocking collectives, heads_split(): return lax.all_to_all(attended, 'seq', 0, 1, tiled=True)  17.2 us
    ppermute x3, starting transfers between devices, heads_split(): lax.ppermute(mine[:, j * width:(j + 1) * width], 'seq', [(s, (3 * s + j)...  10.8 us
    ppermute x3, waiting for transfers between devices, heads_split(): lax.ppermute(mine[:, j * width:(j + 1) * width], 'seq', [(s, (3 * s + j)...  6.42 us
  transfers between devices with their start and end apart: 5, of which 4 were waited for; matrix products, arithmetic and copies ran while one was open for 0% of the time, Pallas kernels for 0%

profile of v1, /device:TPU:0, one launch (start us, length us, event | category | flops | bytes accessed | tf_op | source)
XLA Modules:
  0.0 203.6 jit_solution(11988967125616047798)
XLA Ops:
  6.5 0.0 copy-start
  6.6 0.0 copy-start.2
  6.6 0.0 copy-start.1
  6.6 0.0 copy-start.3
  6.6 0.0 all-gather.5.cloned.1.call-start
  6.6 1.4 constant_dynamic-slice_fusion
  8.0 0.7 collective-permute-start
  8.7 5.8 %collective-permute-start.1 = (bf16[576,256]{1,0:T(8,128)(2,1)S(1)}, bf16[576,256]{1,0:T(8,128)(2,1)S(1)}, u32[]{:S(2)}, u32[]{:S(2)}) collective-permute-start(bf16[576,256]{1,0:T(8,128)(2,1)S(1)} %get-tuple-element.6), channel_id=1, source_target_pairs={{0,4},{4,16},{8,28},{12,8},{16,20},{20,0},{24,12},{28,24},{1,5},{5... | collective-permute-start | bytes 884744 | tf_op jit(solution)/shard_map/ppermute | solution.py:364
  14.5 4.4 %collective-permute-start.2 = (bf16[576,256]{1,0:T(8,128)(2,1)S(1)}, bf16[576,256]{1,0:T(8,128)(2,1)S(1)}, u32[]{:S(2)}, u32[]{:S(2)}) collective-permute-start(bf16[576,256]{1,0:T(8,128)(2,1)S(1)} %get-tuple-element.7), channel_id=1, source_target_pairs={{0,8},{4,20},{8,0},{12,12},{16,24},{20,4},{24,16},{28,28},{1,9},{5... | collective-permute-start | bytes 884744 | tf_op jit(solution)/shard_map/ppermute | solution.py:364
  18.9 0.0 collective-permute-done
  18.9 5.6 %collective-permute-done.1 = bf16[576,256]{1,0:T(8,128)(2,1)S(1)} collective-permute-done((bf16[576,256]{1,0:T(8,128)(2,1)S(1)}, bf16[576,256]{1,0:T(8,128)(2,1)S(1)}, u32[]{:S(2)}, u32[]{:S(2)}) %collective-permute-start.1) | collective-permute-done | bytes 294944 | tf_op jit(solution)/shard_map/ppermute | solution.py:364
  24.4 0.9 collective-permute-done.2
  25.3 1.1 pad_maximum_fusion
  26.4 0.0 all-gather.5.cloned.1.call-update
  26.4 0.0 all-gather.3.cloned.1.call-start
  26.5 0.7 all-gather.3.cloned.1.call-update
  27.2 0.0 copy-done.8
  27.2 0.3 copy.12.bw
  27.5 38.5 %all-gather.5.cloned.1.call-done.w = bf16[3,2304,256]{2,1,0:T(8,128)(2,1)} async-done(((bf16[3,576,256]{2,1,0:T(8,128)(2,1)}), bf16[3,2304,256]{2,1,0:T(8,128)(2,1)}) %all-gather.5.cloned.1.call-update) | async-done | bytes 3538960 | tf_op jit(solution)/shard_map/all_gather | solution.py:367
  66.0 82.1 %all-gather.3.cloned.1.call-done.tok = bf16[1024,2304]{1,0:T(8,128)(2,1)} async-done(((bf16[128,2304]{1,0:T(8,128)(2,1)}), bf16[1024,2304]{1,0:T(8,128)(2,1)}) %all-gather.3.cloned.1.call-update) | async-done | bytes 4718608 | tf_op jit(solution)/shard_map/all_gather | solution.py:361
  148.1 0.0 copy-done.4
  148.2 30.6 %shard_map.109 = bf16[1024,256]{1,0:T(8,128)(2,1)S(1)} custom-call(bf16[1024,2304]{1,0:T(8,128)(2,1)} %all-gather.3.cloned.1.call-done.tok, bf16[3,2304,256]{2,1,0:T(8,128)(2,1)} %all-gather.5.cloned.1.call-done.w, f32[4,6144]{1,0:T(4,128)S(1)} %copy-done.4, bf16[2304,128]{1,0:T(8,128)(2,1)S(1)} %copy-done, bf16[128,2048]{1,0:T(8,128)(2,1)S(1)} %copy-done.2, ...), custom_call_target="tpu_custom_call" | custom-call | tf_op jit(solution)/shard_map/pallas_call | solution.py:371
  178.7 17.2 %all_to_all.19 = bf16[8,128,256]{2,1,0:T(8,128)(2,1)S(1)} all-to-all(bf16[8,128,256]{2,1,0:T(8,128)(2,1)S(1)} %bitcast.10), channel_id=1, replica_groups=mesh['seq'=8,'rep'=4] {'seq'}, dimensions={0} | all-to-all | bytes 1048576 | tf_op jit(solution)/shard_map/all_to_all | solution.py:385
  195.9 0.8 copy.14
  (12 shorter events, 0.0 us)
Async XLA Ops:
  6.5 20.6 %copy-start.8 = (bf16[2304,16]{0,1:T(8,128)(2,1)S(1)}, bf16[2304,16]{0,1:T(8,128)(2,1)}, u32[]{:S(2)}) copy-start(bf16[2304,16]{0,1:T(8,128)(2,1)} %param.17) | copy-start | bytes 221188
  6.5 141.6 %copy-start.5 = (f32[2048]{0:T(1024)S(1)}, f32[2048]{0:T(1024)}, u32[]{:S(2)}) copy-start(f32[2048]{0:T(1024)} %param.16) | copy-start | bytes 24580
  6.5 141.6 %copy-start.6 = (f32[16]{0:T(128)S(1)}, f32[16]{0:T(128)}, u32[]{:S(2)}) copy-start(f32[16]{0:T(128)} %param.18) | copy-start | bytes 196
  6.5 141.6 %copy-start.7 = (f32[128]{0:T(128)S(1)}, f32[128]{0:T(128)}, u32[]{:S(2)}) copy-start(f32[128]{0:T(128)} %param.21) | copy-start | bytes 1540
  6.5 141.6 %copy-start.4 = (f32[4,6144]{1,0:T(4,128)S(1)}, f32[4,6144]{1,0:T(4,128)}, u32[]{:S(2)}) copy-start(f32[4,6144]{1,0:T(4,128)} %conv.1) | copy-start | bytes 294916
  6.5 141.6 %copy-start = (bf16[2304,128]{1,0:T(8,128)(2,1)S(1)}, bf16[2304,128]{1,0:T(8,128)(2,1)}, u32[]{:S(2)}) copy-start(bf16[2304,128]{1,0:T(8,128)(2,1)} %dd.1) | copy-start | bytes 1769476
  6.6 141.6 %copy-start.2 = (bf16[128,2048]{1,0:T(8,128)(2,1)S(1)}, bf16[128,2048]{1,0:T(8,128)(2,1)}, u32[]{:S(2)}) copy-start(bf16[128,2048]{1,0:T(8,128)(2,1)} %du.1) | copy-start | bytes 1572868
  6.6 141.6 %copy-start.1 = (bf16[2304,128]{1,0:T(8,128)(2,1)S(1)}, bf16[2304,128]{1,0:T(8,128)(2,1)}, u32[]{:S(2)}) copy-start(bf16[2304,128]{1,0:T(8,128)(2,1)} %gd.1) | copy-start | bytes 1769476
  6.6 141.6 %copy-start.3 = (bf16[128,2048]{1,0:T(8,128)(2,1)S(1)}, bf16[128,2048]{1,0:T(8,128)(2,1)}, u32[]{:S(2)}) copy-start(bf16[128,2048]{1,0:T(8,128)(2,1)} %gu.1) | copy-start | bytes 1572868
  6.6 59.4 %all-gather.5.cloned.1.call-start = ((), (), s32[]{:S(2)}) async-start(), calls=%async_computation.2 | async-start | bytes 4423680 | tf_op jit(solution)/shard_map/all_gather | solution.py:367
  8.0 10.9 %collective-permute-start = (bf16[576,256]{1,0:T(8,128)(2,1)S(1)}, bf16[576,256]{1,0:T(8,128)(2,1)S(1)}, u32[]{:S(2)}, u32[]{:S(2)}) collective-permute-start(bf16[576,256]{1,0:T(8,128)(2,1)S(1)} %get-tuple-element.5), channel_id=1, source_target_pairs={{0,0},{4,12},{8,24},{12,4},{16,16},{20,28},{24,8},{28,20},{1,1},{5... | collective-permute-start | bytes 884744 | tf_op jit(solution)/shard_map/ppermute | solution.py:364
  8.7 15.8 %collective-permute-start.1 = (bf16[576,256]{1,0:T(8,128)(2,1)S(1)}, bf16[576,256]{1,0:T(8,128)(2,1)S(1)}, u32[]{:S(2)}, u32[]{:S(2)}) collective-permute-start(bf16[576,256]{1,0:T(8,128)(2,1)S(1)} %get-tuple-element.6), channel_id=1, source_target_pairs={{0,4},{4,16},{8,28},{12,8},{16,20},{20,0},{24,12},{28,24},{1,5},{5... | collective-permute-start | bytes 884744 | tf_op jit(solution)/shard_map/ppermute | solution.py:364
  14.5 10.8 %collective-permute-start.2 = (bf16[576,256]{1,0:T(8,128)(2,1)S(1)}, bf16[576,256]{1,0:T(8,128)(2,1)S(1)}, u32[]{:S(2)}, u32[]{:S(2)}) collective-permute-start(bf16[576,256]{1,0:T(8,128)(2,1)S(1)} %get-tuple-element.7), channel_id=1, source_target_pairs={{0,8},{4,20},{8,0},{12,12},{16,24},{20,4},{24,16},{28,28},{1,9},{5... | collective-permute-start | bytes 884744 | tf_op jit(solution)/shard_map/ppermute | solution.py:364
  26.4 121.7 %all-gather.3.cloned.1.call-start = ((), (), s32[]{:S(2)}) async-start(), calls=%async_computation.1 | async-start | bytes 5308416 | tf_op jit(solution)/shard_map/all_gather | solution.py:361
Sparse Core Ops, SparseCore 0:
  26.5 39.4 all-gather.4
  68.2 79.8 all-gather.2

commit v2 on v1

--- a/solution.py
+++ b/solution.py
@@ -322,6 +322,166 @@
     lax.fori_loop(0, chunks, step, 0)
 
 
+MESH = pl.DeviceIdType.MESH
+
+
+def ring_place(device, n):
+    return jnp.where(device % 2 == 0, device // 2, n - 1 - device // 2)
+
+
+def ring_device(place, n):
+    return jnp.where(place < n // 2, 2 * place, 2 * (n - 1 - place) + 1)
+
+
+def greet(n):
+    me, rep = lax.axis_index("seq"), lax.axis_index("rep")
+    barrier = pltpu.get_barrier_semaphore()
+    for k in range(1, n):
+        pl.semaphore_signal(barrier, inc=1, device_id={"seq": (me + k) % n}, device_id_type=MESH)
+    for other in ((rep + 2) % 4, rep + 1 - 2 * (rep % 2)):
+        pl.semaphore_signal(barrier, inc=1, device_id={"rep": other}, device_id_type=MESH)
+    pl.semaphore_wait(barrier, n + 1)
+
+
+def remote(src, dst, sems, k, to):
+    return pltpu.make_async_remote_copy(
+        src_ref=src, dst_ref=dst, send_sem=sems[0].at[k], recv_sem=sems[1].at[k], device_id=to, device_id_type=MESH
+    )
+
+
+def ring_copies(n, blocks, sems):
+    me = lax.axis_index("seq")
+    place = ring_place(me, n)
+    right = {"seq": ring_device((place + 1) % n, n)}
+    left = {"seq": ring_device((place + n - 1) % n, n)}
+    half = blocks.shape[1] // 2
+    steps = []
+    for k in range(n // 2):
+        goes_right = blocks.at[ring_device((place + n - k) % n, n)]
+        goes_left = blocks.at[ring_device((place + k) % n, n)]
+        comes_left = blocks.at[ring_device((place + n - k - 1) % n, n)]
+        comes_right = blocks.at[ring_device((place + k + 1) % n, n)]
+        if k == n // 2 - 1:
+            goes_right, comes_left = goes_right.at[pl.ds(0, half)], comes_left.at[pl.ds(0, half)]
+            goes_left, comes_right = goes_left.at[pl.ds(half, half)], comes_right.at[pl.ds(half, half)]
+        steps.append(
+            (
+                remote(goes_right, goes_right, sems, 2 * k, right),
+                remote(goes_left, goes_left, sems, 2 * k + 1, left),
+                remote(comes_left, comes_left, sems, 2 * k, left),
+                remote(comes_right, comes_right, sems, 2 * k + 1, right),
+            )
+        )
+    return steps
+
+
+class WeightMoves:
+    def __init__(self, n, source, held, sems, local_sems):
+        self.n, self.held = n, held
+        me, rep = lax.axis_index("seq"), lax.axis_index("rep")
+        width = held.shape[2]
+        share = held.shape[1] // 4
+        inverse = pow(3, -1, n)
+        across, beside = (rep + 2) % 4, rep + 1 - 2 * (rep % 2)
+        rows = lambda r: pl.ds(pl.multiple_of(r * share, 16), share)
+        self.out, self.sent_here, self.came_here, self.local = [], [], [], []
+        self.to_across, self.to_beside, self.onward = [], [], []
+        self.from_across, self.from_beside, self.from_onward = [], [], []
+        for j in range(3):
+            piece = source.at[rows(rep), j * width : (j + 1) * width]
+            mine = held.at[j, rows(rep)]
+            to = (3 * me + j) % n
+            self.sent_here.append(to == me)
+            self.came_here.append((inverse * (me + n - j)) % n == me)
+            self.out.append(remote(piece, mine, sems, j, {"seq": to}))
+            self.local.append(pltpu.make_async_copy(piece, mine, local_sems.at[j]))
+            self.to_across.append(remote(mine, mine, sems, 3 + j, {"rep": across}))
+            self.to_beside.append(remote(mine, mine, sems, 6 + j, {"rep": beside}))
+            over = held.at[j, rows(across)]
+            self.from_across.append(remote(over, over, sems, 3 + j, {"rep": across}))
+            self.onward.append(remote(over, over, sems, 9 + j, {"rep": beside}))
+            near = held.at[j, rows(beside)]
+            self.from_beside.append(remote(near, near, sems, 6 + j, {"rep": beside}))
+            far = held.at[j, rows((beside + 2) % 4)]
+            self.from_onward.append(remote(far, far, sems, 9 + j, {"rep": beside}))
+
+    def begin(self):
+        for j in range(3):
+            pl.when(self.sent_here[j])(self.local[j].start)
+            pl.when(jnp.logical_not(self.sent_here[j]))(self.out[j].start)
+
+    def spread(self):
+        for j in range(3):
+            pl.when(self.came_here[j])(self.local[j].wait)
+            pl.when(jnp.logical_not(self.came_here[j]))(self.out[j].wait_recv)
+            self.to_across[j].start()
+            self.to_beside[j].start()
+
+    def pass_on(self):
+        for j in range(3):
+            self.from_across[j].wait_recv()
+            self.onward[j].start()
+
+    def finish(self):
+        for j in range(3):
+            self.from_beside[j].wait_recv()
+            self.from_onward[j].wait_recv()
+
+    def sent(self):
+        for j in range(3):
+            pl.when(jnp.logical_not(self.sent_here[j]))(self.out[j].wait_send)
+            self.to_across[j].wait_send()
+            self.to_beside[j].wait_send()
+            self.onward[j].wait_send()
+
+
+def gather_kernel(n, tok, w, blocks, held, tok_send, tok_recv, w_send, w_recv, local):
+    me = lax.axis_index("seq")
+    own = pltpu.make_async_copy(tok, blocks.at[me], local.at[3])
+    own.start()
+    greet(n)
+    moves = WeightMoves(n, w, held, (w_send, w_recv), local)
+    moves.begin()
+    own.wait()
+    steps = ring_copies(n, blocks, (tok_send, tok_recv))
+    for k, (right, left, came_left, came_right) in enumerate(steps):
+        right.start()
+        left.start()
+        if k == 0:
+            moves.spread()
+        if k == 1:
+            moves.pass_on()
+        came_left.wait_recv()
+        came_right.wait_recv()
+    moves.finish()
+    moves.sent()
+    for right, left, came_left, came_right in steps:
+        right.wait_send()
+        left.wait_send()
+
+
+def gathered(tokens, qkv_weight, n, width):
+    depth = qkv_weight.shape[0]
+    anywhere = pl.BlockSpec(memory_space=pl.ANY)
+    return pl.pallas_call(
+        functools.partial(gather_kernel, n),
+        out_shape=[
+            jax.ShapeDtypeStruct((n,) + tokens.shape, tokens.dtype),
+            jax.ShapeDtypeStruct((3, depth, width), qkv_weight.dtype),
+        ],
+        in_specs=[anywhere] * 2,
+        out_specs=[anywhere] * 2,
+        scratch_shapes=[
+            pltpu.SemaphoreType.DMA((n,)),
+            pltpu.SemaphoreType.DMA((n,)),
+            pltpu.SemaphoreType.DMA((12,)),
+            pltpu.SemaphoreType.DMA((12,)),
+            pltpu.SemaphoreType.DMA((4,)),
+        ],
+        compiler_params=pltpu.CompilerParams(collective_id=0, has_side_effects=True),
+    )(tokens, qkv_weight)
+
+
 def heads_kernel(n, heads, tok, w, conv, dd, du, rate, bw, bs, gd, gu, gain, out, mixed_s, low_s, beta_s, m_s, b_s, p_s, q_s, states):
     me = lax.axis_index("seq")
     count = tok.shape[0]
@@ -352,19 +512,11 @@
 
 
 def heads_split(tokens, qkv_weight, conv_weight, decay_down, decay_up, decay_rate, beta_weight, beta_scale, gate_down, gate_up, norm_gain):
-    n, reps = lax.axis_size("seq"), lax.axis_size("rep")
-    rep = lax.axis_index("rep")
-    depth = qkv_weight.shape[0]
+    n = lax.axis_size("seq")
     heads = H // n
     width = heads * DK
-    share = depth // reps
-    everything = lax.all_gather(tokens, "seq", axis=0, tiled=True)
-    mine = lax.dynamic_slice_in_dim(qkv_weight, rep * share, share, 0)
-    pieces = [
-        lax.ppermute(mine[:, j * width : (j + 1) * width], "seq", [(s, (3 * s + j) % n) for s in range(n)])
-        for j in range(3)
-    ]
-    weight = lax.all_gather(jnp.stack(pieces), "rep", axis=1, tiled=True)
+    blocks, weight = gathered(tokens, qkv_weight, n, width)
+    everything = blocks.reshape(-1, tokens.shape[1])
     count = everything.shape[0]
     slots = count // CHUNK * heads
     square = pltpu.VMEM((slots, DK, DK), jnp.float32)
@@ -387,7 +539,7 @@
 
 def by_heads(mesh):
     n, reps = mesh.shape["seq"], mesh.shape["rep"]
-    return H % n == 0 and n % 3 != 0
+    return H % n == 0 and n % 3 != 0 and n % 2 == 0 and reps == 4
 
 
 def solution(mesh):

time: 204 us -> 125 us (0.61)
  waiting for transfers between devices: 128 us -> 0 us
  Pallas kernels: 30.6 us -> 106 us
  between operations: 13.5 us -> 0.11 us
  starting transfers between devices: 10.9 us -> 0 us
    all_gather x2 -> x0, waiting for transfers between devices: 121 us -> none  [the longest x1 82.1 us: heads_split(): everything = lax.all_gather(tokens, 'seq', axis=0, tiled=True)]
    pallas_call x0 -> x1, Pallas kernels: none -> 75.8 us  [gathered(): pl.pallas_call(functools.partial(gather_kernel, n), out_shape=[jax.ShapeD...]
    ppermute x3 -> x0, starting transfers between devices: 10.8 us -> none  [heads_split(): lax.ppermute(mine[:, j * width:(j + 1) * width], 'seq', [(s, (3 * s + j)...]
    ppermute x3 -> x0, waiting for transfers between devices: 6.42 us -> none  [heads_split(): lax.ppermute(mine[:, j * width:(j + 1) * width], 'seq', [(s, (3 * s + j)...]
  transfers between devices with their start and end apart: 5 -> 0, of which waited for: 4 -> 0; matrix products, arithmetic and copies ran while one was open for 0% -> 0% of each run, Pallas kernels for 0% -> 0%
where the time goes in v2:
time: 125 us
  Pallas kernels  106 us (85%)
  blocking collectives  16 us (13%)
  local copies, waits for them, and re-layouts  2.23 us (2%)
    pallas_call x1, Pallas kernels, gathered(): pl.pallas_call(functools.partial(gather_kernel, n), out_shape=[jax.ShapeD...  75.8 us
    pallas_call x1, Pallas kernels, heads_split(): pl.pallas_call(functools.partial(heads_kernel, n, heads), out_shape=jax.S...  30.6 us
    all_to_all x1, blocking collectives, heads_split(): return lax.all_to_all(attended, 'seq', 0, 1, tiled=True)  16 us

profile of v2, /device:TPU:0, one launch (start us, length us, event | category | flops | bytes accessed | tf_op | source)
XLA Modules:
  0.0 124.7 jit_solution(4774197829258010271)
XLA Ops:
  0.0 0.0 copy-start.7
  0.0 0.0 copy-start.3
  0.0 0.0 copy-start.1
  0.0 0.0 copy-start.6
  0.0 0.0 copy-start.5
  0.0 0.0 copy-start.2
  0.0 0.0 copy-start
  0.0 0.0 copy-start.4
  0.0 1.4 %copy.12.bw = bf16[2304,16]{1,0:T(8,128)(2,1)S(1)} copy(bf16[2304,16]{0,1:T(8,128)(2,1)} %param.17) | data formatting | bytes 147456 | tf_op args[6]
  1.4 75.8 %shard_map.109 = (bf16[8,128,2304]{2,1,0:T(8,128)(2,1)}, bf16[3,2304,256]{2,1,0:T(8,128)(2,1)}) custom-call(bf16[128,2304]{1,0:T(8,128)(2,1)} %tok.1, bf16[2304,768]{1,0:T(8,128)(2,1)} %w.1), custom_call_target="tpu_custom_call" | custom-call | tf_op jit(solution)/shard_map/pallas_call | solution.py:466
  77.2 0.0 copy-done.7
  77.2 0.0 copy-done.3
  77.2 0.0 copy-done.1
  77.2 0.0 copy-done.6
  77.2 0.0 copy-done.5
  77.2 0.0 copy-done.2
  77.3 0.0 copy-done
  77.3 0.0 copy-done.4
  77.3 30.6 %shard_map.110 = bf16[1024,256]{1,0:T(8,128)(2,1)S(1)} custom-call(bf16[1024,2304]{1,0:T(8,128)(2,1)} %bitcast.12, bf16[3,2304,256]{2,1,0:T(8,128)(2,1)} %get-tuple-element.8.w, f32[4,6144]{1,0:T(4,128)S(1)} %copy-done.4, bf16[2304,128]{1,0:T(8,128)(2,1)S(1)} %copy-done, bf16[128,2048]{1,0:T(8,128)(2,1)S(1)} %copy-done.2, f32[1,2048]{1,0:T(1,128)S(1)} %bitcast.9, ...), custom_call_target="tpu_custom_call" | custom-call | tf_op jit(solution)/shard_map/pallas_call | solution.py:523
  107.8 16.0 %all_to_all.19 = bf16[8,128,256]{2,1,0:T(8,128)(2,1)S(1)} all-to-all(bf16[8,128,256]{2,1,0:T(8,128)(2,1)S(1)} %bitcast.8), channel_id=1, replica_groups=mesh['seq'=8,'rep'=4] {'seq'}, dimensions={0} | all-to-all | bytes 1048576 | tf_op jit(solution)/shard_map/all_to_all | solution.py:537
  123.9 0.8 copy.14
Async XLA Ops:
  0.0 77.2 %copy-start.7 = (f32[128]{0:T(128)S(1)}, f32[128]{0:T(128)}, u32[]{:S(2)}) copy-start(f32[128]{0:T(128)} %param.21) | copy-start | bytes 1540
  0.0 77.2 %copy-start.3 = (bf16[128,2048]{1,0:T(8,128)(2,1)S(1)}, bf16[128,2048]{1,0:T(8,128)(2,1)}, u32[]{:S(2)}) copy-start(bf16[128,2048]{1,0:T(8,128)(2,1)} %gu.1) | copy-start | bytes 1572868
  0.0 77.2 %copy-start.1 = (bf16[2304,128]{1,0:T(8,128)(2,1)S(1)}, bf16[2304,128]{1,0:T(8,128)(2,1)}, u32[]{:S(2)}) copy-start(bf16[2304,128]{1,0:T(8,128)(2,1)} %gd.1) | copy-start | bytes 1769476
  0.0 77.2 %copy-start.6 = (f32[16]{0:T(128)S(1)}, f32[16]{0:T(128)}, u32[]{:S(2)}) copy-start(f32[16]{0:T(128)} %param.18) | copy-start | bytes 196
  0.0 77.2 %copy-start.5 = (f32[2048]{0:T(1024)S(1)}, f32[2048]{0:T(1024)}, u32[]{:S(2)}) copy-start(f32[2048]{0:T(1024)} %param.16) | copy-start | bytes 24580
  0.0 77.2 %copy-start.2 = (bf16[128,2048]{1,0:T(8,128)(2,1)S(1)}, bf16[128,2048]{1,0:T(8,128)(2,1)}, u32[]{:S(2)}) copy-start(bf16[128,2048]{1,0:T(8,128)(2,1)} %du.1) | copy-start | bytes 1572868
  0.0 77.2 %copy-start = (bf16[2304,128]{1,0:T(8,128)(2,1)S(1)}, bf16[2304,128]{1,0:T(8,128)(2,1)}, u32[]{:S(2)}) copy-start(bf16[2304,128]{1,0:T(8,128)(2,1)} %dd.1) | copy-start | bytes 1769476
  0.0 77.2 %copy-start.4 = (f32[4,6144]{1,0:T(4,128)S(1)}, f32[4,6144]{1,0:T(4,128)}, u32[]{:S(2)}) copy-start(f32[4,6144]{1,0:T(4,128)} %conv.1) | copy-start | bytes 294916

commit v3 on v2

--- a/solution.py
+++ b/solution.py
@@ -208,7 +208,7 @@
     return split, mm3
 
 
-LEVELS = {"g": 3, "t": 1, "s": 3, "m": 3, "c": 3}
+LEVELS = {"g": 1, "t": 1, "s": 1, "m": 3, "c": 3}
 
 
 def sigmoid(u):
@@ -449,7 +449,7 @@
         left.start()
         if k == 0:
             moves.spread()
-        if k == 1:
+        if k == 2:
             moves.pass_on()
         came_left.wait_recv()
         came_right.wait_recv()

time: 125 us -> 124 us (level)
  no operation moved by 1% of the time
where the time goes in v3:
time: 124 us
  Pallas kernels  105 us (85%)
  blocking collectives  16 us (13%)
  local copies, waits for them, and re-layouts  2.23 us (2%)
    pallas_call x1, Pallas kernels, gathered(): pl.pallas_call(functools.partial(gather_kernel, n), out_shape=[jax.ShapeD...  75.8 us
    pallas_call x1, Pallas kernels, heads_split(): pl.pallas_call(functools.partial(heads_kernel, n, heads), out_shape=jax.S...  29.4 us
    all_to_all x1, blocking collectives, heads_split(): return lax.all_to_all(attended, 'seq', 0, 1, tiled=True)  16 us

profile of v3, /device:TPU:0, one launch (start us, length us, event | category | flops | bytes accessed | tf_op | source)
XLA Modules:
  0.0 123.6 jit_solution(9334788621341072366)
XLA Ops:
  0.0 0.0 copy-start.7
  0.0 0.0 copy-start.3
  0.0 0.0 copy-start.1
  0.0 0.0 copy-start.6
  0.0 0.0 copy-start.5
  0.0 0.0 copy-start.2
  0.0 0.0 copy-start
  0.0 0.0 copy-start.4
  0.0 1.4 %copy.12.bw = bf16[2304,16]{1,0:T(8,128)(2,1)S(1)} copy(bf16[2304,16]{0,1:T(8,128)(2,1)} %param.17) | data formatting | bytes 147456 | tf_op args[6]
  1.4 75.8 %shard_map.109 = (bf16[8,128,2304]{2,1,0:T(8,128)(2,1)}, bf16[3,2304,256]{2,1,0:T(8,128)(2,1)}) custom-call(bf16[128,2304]{1,0:T(8,128)(2,1)} %tok.1, bf16[2304,768]{1,0:T(8,128)(2,1)} %w.1), custom_call_target="tpu_custom_call" | custom-call | tf_op jit(solution)/shard_map/pallas_call | solution.py:466
  77.2 0.0 copy-done.7
  77.2 0.0 copy-done.3
  77.2 0.0 copy-done.1
  77.2 0.0 copy-done.6
  77.2 0.0 copy-done.5
  77.2 0.0 copy-done.2
  77.3 0.0 copy-done
  77.3 0.0 copy-done.4
  77.3 29.4 %shard_map.110 = bf16[1024,256]{1,0:T(8,128)(2,1)S(1)} custom-call(bf16[1024,2304]{1,0:T(8,128)(2,1)} %bitcast.12, bf16[3,2304,256]{2,1,0:T(8,128)(2,1)} %get-tuple-element.8.w, f32[4,6144]{1,0:T(4,128)S(1)} %copy-done.4, bf16[2304,128]{1,0:T(8,128)(2,1)S(1)} %copy-done, bf16[128,2048]{1,0:T(8,128)(2,1)S(1)} %copy-done.2, f32[1,2048]{1,0:T(1,128)S(1)} %bitcast.9, ...), custom_call_target="tpu_custom_call" | custom-call | tf_op jit(solution)/shard_map/pallas_call | solution.py:523
  106.7 16.0 %all_to_all.19 = bf16[8,128,256]{2,1,0:T(8,128)(2,1)S(1)} all-to-all(bf16[8,128,256]{2,1,0:T(8,128)(2,1)S(1)} %bitcast.8), channel_id=1, replica_groups=mesh['seq'=8,'rep'=4] {'seq'}, dimensions={0} | all-to-all | bytes 1048576 | tf_op jit(solution)/shard_map/all_to_all | solution.py:537
  122.7 0.8 copy.14
Async XLA Ops:
  0.0 77.2 %copy-start.7 = (f32[128]{0:T(128)S(1)}, f32[128]{0:T(128)}, u32[]{:S(2)}) copy-start(f32[128]{0:T(128)} %param.21) | copy-start | bytes 1540
  0.0 77.2 %copy-start.3 = (bf16[128,2048]{1,0:T(8,128)(2,1)S(1)}, bf16[128,2048]{1,0:T(8,128)(2,1)}, u32[]{:S(2)}) copy-start(bf16[128,2048]{1,0:T(8,128)(2,1)} %gu.1) | copy-start | bytes 1572868
  0.0 77.2 %copy-start.1 = (bf16[2304,128]{1,0:T(8,128)(2,1)S(1)}, bf16[2304,128]{1,0:T(8,128)(2,1)}, u32[]{:S(2)}) copy-start(bf16[2304,128]{1,0:T(8,128)(2,1)} %gd.1) | copy-start | bytes 1769476
  0.0 77.2 %copy-start.6 = (f32[16]{0:T(128)S(1)}, f32[16]{0:T(128)}, u32[]{:S(2)}) copy-start(f32[16]{0:T(128)} %param.18) | copy-start | bytes 196
  0.0 77.2 %copy-start.5 = (f32[2048]{0:T(1024)S(1)}, f32[2048]{0:T(1024)}, u32[]{:S(2)}) copy-start(f32[2048]{0:T(1024)} %param.16) | copy-start | bytes 24580
  0.0 77.2 %copy-start.2 = (bf16[128,2048]{1,0:T(8,128)(2,1)S(1)}, bf16[128,2048]{1,0:T(8,128)(2,1)}, u32[]{:S(2)}) copy-start(bf16[128,2048]{1,0:T(8,128)(2,1)} %du.1) | copy-start | bytes 1572868
  0.0 77.2 %copy-start = (bf16[2304,128]{1,0:T(8,128)(2,1)S(1)}, bf16[2304,128]{1,0:T(8,128)(2,1)}, u32[]{:S(2)}) copy-start(bf16[2304,128]{1,0:T(8,128)(2,1)} %dd.1) | copy-start | bytes 1769476
  0.0 77.2 %copy-start.4 = (f32[4,6144]{1,0:T(4,128)S(1)}, f32[4,6144]{1,0:T(4,128)}, u32[]{:S(2)}) copy-start(f32[4,6144]{1,0:T(4,128)} %conv.1) | copy-start | bytes 294916

commit v4 on v3

--- a/solution.py
+++ b/solution.py
@@ -208,7 +208,7 @@
     return split, mm3
 
 
-LEVELS = {"g": 1, "t": 1, "s": 1, "m": 3, "c": 3}
+LEVELS = {"g": 3, "t": 1, "s": 3, "m": 3, "c": 3}
 
 
 def sigmoid(u):
@@ -298,7 +298,7 @@
         b_s[slot] = dot(ec, vc, TN)
 
 
-def run_states(chunks, me, heads, refs, low_s, terms, states, put):
+def run_states(chunks, me, heads, refs, low_s, terms, states, put, post):
     gu, gain = refs
     m_s, b_s, p_s, q_s = terms
     C = CHUNK
@@ -317,6 +317,7 @@
             gate = sigmoid(mm(low_s[pl.ds(pl.multiple_of(chunk * C, C), C), DK:], gu[:, pl.ds(at, DK)]))
             core = core * lax.rsqrt(jnp.mean(core * core, axis=-1, keepdims=True) + 1e-06) * gain[...]
             put(chunk, h, low(core * gate))
+        post(chunk)
         return carry
 
     lax.fori_loop(0, chunks, step, 0)
@@ -482,10 +483,12 @@
     )(tokens, qkv_weight)
 
 
-def heads_kernel(n, heads, tok, w, conv, dd, du, rate, bw, bs, gd, gu, gain, out, mixed_s, low_s, beta_s, m_s, b_s, p_s, q_s, states):
+def heads_kernel(n, heads, tok, w, conv, dd, du, rate, bw, bs, gd, gu, gain, out, mixed_s, low_s, beta_s, m_s, b_s, p_s, q_s, states, stage, send, recv, local):
     me = lax.axis_index("seq")
     count = tok.shape[0]
     chunks = count // CHUNK
+    width = heads * DK
+    greet(n)
     mixed_s[0:8, :] = jnp.zeros((8, mixed_s.shape[1]), jnp.float32)
 
     def w_at(t):
@@ -505,10 +508,32 @@
 
     lax.fori_loop(0, chunks // 2, second, 0)
 
+    def columns(device):
+        return out.at[:, pl.ds(pl.multiple_of(device * width, width), width)]
+
+    def parcel(to):
+        return pltpu.make_async_remote_copy(
+            src_ref=stage.at[to], dst_ref=columns(me), send_sem=send.at[to], recv_sem=recv.at[me],
+            device_id={"seq": to}, device_id_type=MESH,
+        )
+
     def put(chunk, h, value):
-        out[pl.ds(pl.multiple_of(chunk * CHUNK, CHUNK), CHUNK), h * DK : (h + 1) * DK] = value
-
-    run_states(chunks, me, heads, (gu, gain), low_s, (m_s, b_s, p_s, q_s), states, put)
+        stage[chunk, :, h * DK : (h + 1) * DK] = value
+
+    def post(chunk):
+        pl.when(chunk != me)(lambda: parcel(chunk).start())
+
+    run_states(chunks, me, heads, (gu, gain), low_s, (m_s, b_s, p_s, q_s), states, put, post)
+    own = pltpu.make_async_copy(stage.at[me], columns(me), local.at[0])
+    own.start()
+    own.wait()
+    for k in range(1, n):
+        other = (me + k) % n
+        parcel(other).wait_send()
+        pltpu.make_async_remote_copy(
+            src_ref=stage.at[other], dst_ref=columns(other), send_sem=send.at[other], recv_sem=recv.at[other],
+            device_id={"seq": other}, device_id_type=MESH,
+        ).wait_recv()
 
 
 def heads_split(tokens, qkv_weight, conv_weight, decay_down, decay_up, decay_rate, beta_weight, beta_scale, gate_down, gate_up, norm_gain):
@@ -522,7 +547,7 @@
     square = pltpu.VMEM((slots, DK, DK), jnp.float32)
     attended = pl.pallas_call(
         functools.partial(heads_kernel, n, heads),
-        out_shape=jax.ShapeDtypeStruct((count, width), jnp.bfloat16),
+        out_shape=jax.ShapeDtypeStruct((tokens.shape[0], H * DK), jnp.bfloat16),
         in_specs=[pl.BlockSpec(memory_space=pltpu.VMEM)] * 11,
         out_specs=pl.BlockSpec(memory_space=pltpu.VMEM),
         scratch_shapes=[
@@ -531,15 +556,20 @@
             pltpu.VMEM((count, H), jnp.float32),
             square, square, square, square,
             pltpu.VMEM((heads, DK, DK), jnp.float32),
+            pltpu.VMEM((n, CHUNK, width), jnp.bfloat16),
+            pltpu.SemaphoreType.DMA((n,)),
+            pltpu.SemaphoreType.DMA((n,)),
+            pltpu.SemaphoreType.DMA((1,)),
         ],
-        compiler_params=pltpu.CompilerParams(vmem_limit_bytes=48 * 2**20),
+        compiler_params=pltpu.CompilerParams(collective_id=1, has_side_effects=True, vmem_limit_bytes=48 * 2**20),
     )(everything, weight, conv_weight, decay_down, decay_up, decay_rate.reshape(1, -1), beta_weight, beta_scale.reshape(1, -1), gate_down, gate_up, norm_gain.reshape(1, -1))
-    return lax.all_to_all(attended, "seq", 0, 1, tiled=True)
-
-
-def by_heads(mesh):
-    n, reps = mesh.shape["seq"], mesh.shape["rep"]
-    return H % n == 0 and n % 3 != 0 and n % 2 == 0 and reps == 4
+    return attended
+
+
+def layer(tokens, *rest):
+    n, reps = lax.axis_size("seq"), lax.axis_size("rep")
+    fits = H % n == 0 and n % 3 != 0 and n % 2 == 0 and reps == 4 and tokens.shape[0] == CHUNK
+    return (heads_split if fits else tokens_split)(tokens, *rest)
 
 
 def solution(mesh):
@@ -558,5 +588,5 @@
     )
     out_specs = P(("rep", "seq"), None)
     return jax.shard_map(
-        heads_split if by_heads(mesh) else tokens_split, mesh=mesh, in_specs=in_specs, out_specs=out_specs, check_vma=False
-    )
+        layer, mesh=mesh, in_specs=in_specs, out_specs=out_specs, check_vma=False
+    )

time: 124 us -> 119 us (0.960)
  blocking collectives: 16 us -> 0 us
  Pallas kernels: 105 us -> 115 us
    all_to_all x1 -> x0, blocking collectives: 16 us -> none  [heads_split(): return lax.all_to_all(attended, 'seq', 0, 1, tiled=True)]
    pallas_call x1, Pallas kernels: 29.4 us -> 39.3 us  [heads_split(): pl.pallas_call(functools.partial(heads_kernel, n, heads), out_shape=jax.S...]
where the time goes in v4:
time: 119 us; the launch traced here: 117 us
  Pallas kernels  115 us (97%)
  local copies, waits for them, and re-layouts  2.18 us (2%)
    pallas_call x1, Pallas kernels, gathered(): pl.pallas_call(functools.partial(gather_kernel, n), out_shape=[jax.ShapeD...  75.8 us
    pallas_call x1, Pallas kernels, heads_split(): pl.pallas_call(functools.partial(heads_kernel, n, heads), out_shape=jax.S...  39.3 us

profile of v4, /device:TPU:0, one launch (start us, length us, event | category | flops | bytes accessed | tf_op | source)
XLA Modules:
  0.0 117.4 jit_solution(9358618436461306090)
XLA Ops:
  0.0 0.0 copy-start.7
  0.0 0.0 copy-start.3
  0.0 0.0 copy-start.1
  0.0 0.0 copy-start.6
  0.0 0.0 copy-start.5
  0.0 0.0 copy-start.2
  0.0 0.0 copy-start
  0.0 0.0 copy-start.4
  0.0 1.4 %copy.12.bw = bf16[2304,16]{1,0:T(8,128)(2,1)S(1)} copy(bf16[2304,16]{0,1:T(8,128)(2,1)} %param.17) | data formatting | bytes 147456 | tf_op args[6]
  1.4 75.8 %shard_map.109 = (bf16[8,128,2304]{2,1,0:T(8,128)(2,1)}, bf16[3,2304,256]{2,1,0:T(8,128)(2,1)}) custom-call(bf16[128,2304]{1,0:T(8,128)(2,1)} %tok.1, bf16[2304,768]{1,0:T(8,128)(2,1)} %w.1), custom_call_target="tpu_custom_call" | custom-call | tf_op jit(solution)/shard_map/pallas_call | solution.py:467
  77.2 0.0 copy-done.7
  77.2 0.0 copy-done.3
  77.2 0.0 copy-done.1
  77.2 0.0 copy-done.6
  77.2 0.0 copy-done.5
  77.2 0.0 copy-done.2
  77.3 0.0 copy-done
  77.3 0.0 copy-done.4
  77.3 39.3 %shard_map.110 = bf16[128,2048]{1,0:T(8,128)(2,1)S(1)} custom-call(bf16[1024,2304]{1,0:T(8,128)(2,1)} %bitcast.7, bf16[3,2304,256]{2,1,0:T(8,128)(2,1)} %get-tuple-element.8.w, f32[4,6144]{1,0:T(4,128)S(1)} %copy-done.4, bf16[2304,128]{1,0:T(8,128)(2,1)S(1)} %copy-done, bf16[128,2048]{1,0:T(8,128)(2,1)S(1)} %copy-done.2, f32[1,2048]{1,0:T(1,128)S(1)} %bitcast.4, ...), custom_call_target="tpu_custom_call" | custom-call | tf_op jit(solution)/shard_map/pallas_call | solution.py:548
  116.6 0.8 copy.14
Async XLA Ops:
  0.0 77.2 %copy-start.7 = (f32[128]{0:T(128)S(1)}, f32[128]{0:T(128)}, u32[]{:S(2)}) copy-start(f32[128]{0:T(128)} %param.21) | copy-start | bytes 1540
  0.0 77.2 %copy-start.3 = (bf16[128,2048]{1,0:T(8,128)(2,1)S(1)}, bf16[128,2048]{1,0:T(8,128)(2,1)}, u32[]{:S(2)}) copy-start(bf16[128,2048]{1,0:T(8,128)(2,1)} %gu.1) | copy-start | bytes 1572868
  0.0 77.2 %copy-start.1 = (bf16[2304,128]{1,0:T(8,128)(2,1)S(1)}, bf16[2304,128]{1,0:T(8,128)(2,1)}, u32[]{:S(2)}) copy-start(bf16[2304,128]{1,0:T(8,128)(2,1)} %gd.1) | copy-start | bytes 1769476
  0.0 77.2 %copy-start.6 = (f32[16]{0:T(128)S(1)}, f32[16]{0:T(128)}, u32[]{:S(2)}) copy-start(f32[16]{0:T(128)} %param.18) | copy-start | bytes 196
  0.0 77.2 %copy-start.5 = (f32[2048]{0:T(1024)S(1)}, f32[2048]{0:T(1024)}, u32[]{:S(2)}) copy-start(f32[2048]{0:T(1024)} %param.16) | copy-start | bytes 24580
  0.0 77.2 %copy-start.2 = (bf16[128,2048]{1,0:T(8,128)(2,1)S(1)}, bf16[128,2048]{1,0:T(8,128)(2,1)}, u32[]{:S(2)}) copy-start(bf16[128,2048]{1,0:T(8,128)(2,1)} %du.1) | copy-start | bytes 1572868
  0.0 77.2 %copy-start = (bf16[2304,128]{1,0:T(8,128)(2,1)S(1)}, bf16[2304,128]{1,0:T(8,128)(2,1)}, u32[]{:S(2)}) copy-start(bf16[2304,128]{1,0:T(8,128)(2,1)} %dd.1) | copy-start | bytes 1769476
  0.0 77.2 %copy-start.4 = (f32[4,6144]{1,0:T(4,128)S(1)}, f32[4,6144]{1,0:T(4,128)}, u32[]{:S(2)}) copy-start(f32[4,6144]{1,0:T(4,128)} %conv.1) | copy-start | bytes 294916

commit v5 on v4

--- a/solution.py
+++ b/solution.py
@@ -304,10 +304,8 @@
     C = CHUNK
     width = heads * DK
     cut, dot = product(LEVELS["c"])
-    for h in range(heads):
-        states[h] = jnp.zeros((DK, DK), jnp.float32)
-
-    def step(chunk, carry):
+
+    def step(chunk):
         for h in range(heads):
             slot = chunk * heads + h
             s = cut(states[h])
@@ -318,9 +316,9 @@
             core = core * lax.rsqrt(jnp.mean(core * core, axis=-1, keepdims=True) + 1e-06) * gain[...]
             put(chunk, h, low(core * gate))
         post(chunk)
-        return carry
-
-    lax.fori_loop(0, chunks, step, 0)
+
+    for chunk in chunks:
+        step(chunk)
 
 
 MESH = pl.DeviceIdType.MESH
@@ -501,13 +499,6 @@
 
     lax.fori_loop(0, chunks, first, 0)
 
-    def second(c, carry):
-        places = [(c * 2 + i, h) for i in range(2) for h in range(heads)]
-        chunk_terms(places, me, heads, (conv, du, rate), (mixed_s, low_s, beta_s), (m_s, b_s, p_s, q_s))
-        return carry
-
-    lax.fori_loop(0, chunks // 2, second, 0)
-
     def columns(device):
         return out.at[:, pl.ds(pl.multiple_of(device * width, width), width)]
 
@@ -523,7 +514,18 @@
     def post(chunk):
         pl.when(chunk != me)(lambda: parcel(chunk).start())
 
-    run_states(chunks, me, heads, (gu, gain), low_s, (m_s, b_s, p_s, q_s), states, put, post)
+    for h in range(heads):
+        states[h] = jnp.zeros((DK, DK), jnp.float32)
+
+    def second(c, carry):
+        pair = [c * 2, c * 2 + 1]
+        terms = (m_s, b_s, p_s, q_s)
+        places = [(chunk, h) for chunk in pair for h in range(heads)]
+        chunk_terms(places, me, heads, (conv, du, rate), (mixed_s, low_s, beta_s), terms)
+        run_states(pair, me, heads, (gu, gain), low_s, terms, states, put, post)
+        return carry
+
+    lax.fori_loop(0, chunks // 2, second, 0)
     own = pltpu.make_async_copy(stage.at[me], columns(me), local.at[0])
     own.start()
     own.wait()

time: 119 us -> 116 us (0.975)
  the two profiles are of different devices: /device:TPU:0 before, /device:TPU:30 now
where the time goes in v5:
time: 116 us
  Pallas kernels  113 us (97%)
  local copies, waits for them, and re-layouts  2.18 us (2%)
    pallas_call x1, Pallas kernels, gathered(): pl.pallas_call(functools.partial(gather_kernel, n), out_shape=[jax.ShapeD...  72.2 us
    pallas_call x1, Pallas kernels, heads_split(): pl.pallas_call(functools.partial(heads_kernel, n, heads), out_shape=jax.S...  41.3 us

profile of v5, /device:TPU:30, one launch (start us, length us, event | category | flops | bytes accessed | tf_op | source)
XLA Modules:
  0.0 115.8 jit_solution(17177049000214755986)
XLA Ops:
  0.0 0.0 copy-start.7
  0.0 0.0 copy-start.3
  0.0 0.0 copy-start.1
  0.0 0.0 copy-start.6
  0.0 0.0 copy-start.5
  0.0 0.0 copy-start.2
  0.0 0.0 copy-start
  0.0 0.0 copy-start.4
  0.1 1.4 %copy.12.bw = bf16[2304,16]{1,0:T(8,128)(2,1)S(1)} copy(bf16[2304,16]{0,1:T(8,128)(2,1)} %param.17) | data formatting | bytes 147456 | tf_op args[6]
  1.4 72.2 %shard_map.109 = (bf16[8,128,2304]{2,1,0:T(8,128)(2,1)}, bf16[3,2304,256]{2,1,0:T(8,128)(2,1)}) custom-call(bf16[128,2304]{1,0:T(8,128)(2,1)} %tok.1, bf16[2304,768]{1,0:T(8,128)(2,1)} %w.1), custom_call_target="tpu_custom_call" | custom-call | tf_op jit(solution)/shard_map/pallas_call | solution.py:465
  73.6 0.0 copy-done.7
  73.6 0.0 copy-done.3
  73.6 0.0 copy-done.1
  73.6 0.0 copy-done.6
  73.6 0.0 copy-done.5
  73.6 0.0 copy-done.2
  73.6 0.0 copy-done
  73.7 0.0 copy-done.4
  73.7 41.3 %shard_map.110 = bf16[128,2048]{1,0:T(8,128)(2,1)S(1)} custom-call(bf16[1024,2304]{1,0:T(8,128)(2,1)} %bitcast.7, bf16[3,2304,256]{2,1,0:T(8,128)(2,1)} %get-tuple-element.8.w, f32[4,6144]{1,0:T(4,128)S(1)} %copy-done.4, bf16[2304,128]{1,0:T(8,128)(2,1)S(1)} %copy-done, bf16[128,2048]{1,0:T(8,128)(2,1)S(1)} %copy-done.2, f32[1,2048]{1,0:T(1,128)S(1)} %bitcast.4, ...), custom_call_target="tpu_custom_call" | custom-call | tf_op jit(solution)/shard_map/pallas_call | solution.py:550
  115.0 0.8 copy.14
Async XLA Ops:
  0.0 73.6 %copy-start.7 = (f32[128]{0:T(128)S(1)}, f32[128]{0:T(128)}, u32[]{:S(2)}) copy-start(f32[128]{0:T(128)} %param.21) | copy-start | bytes 1540
  0.0 73.6 %copy-start.3 = (bf16[128,2048]{1,0:T(8,128)(2,1)S(1)}, bf16[128,2048]{1,0:T(8,128)(2,1)}, u32[]{:S(2)}) copy-start(bf16[128,2048]{1,0:T(8,128)(2,1)} %gu.1) | copy-start | bytes 1572868
  0.0 73.6 %copy-start.1 = (bf16[2304,128]{1,0:T(8,128)(2,1)S(1)}, bf16[2304,128]{1,0:T(8,128)(2,1)}, u32[]{:S(2)}) copy-start(bf16[2304,128]{1,0:T(8,128)(2,1)} %gd.1) | copy-start | bytes 1769476
  0.0 73.6 %copy-start.6 = (f32[16]{0:T(128)S(1)}, f32[16]{0:T(128)}, u32[]{:S(2)}) copy-start(f32[16]{0:T(128)} %param.18) | copy-start | bytes 196
  0.0 73.6 %copy-start.5 = (f32[2048]{0:T(1024)S(1)}, f32[2048]{0:T(1024)}, u32[]{:S(2)}) copy-start(f32[2048]{0:T(1024)} %param.16) | copy-start | bytes 24580
  0.0 73.6 %copy-start.2 = (bf16[128,2048]{1,0:T(8,128)(2,1)S(1)}, bf16[128,2048]{1,0:T(8,128)(2,1)}, u32[]{:S(2)}) copy-start(bf16[128,2048]{1,0:T(8,128)(2,1)} %du.1) | copy-start | bytes 1572868
  0.0 73.6 %copy-start = (bf16[2304,128]{1,0:T(8,128)(2,1)S(1)}, bf16[2304,128]{1,0:T(8,128)(2,1)}, u32[]{:S(2)}) copy-start(bf16[2304,128]{1,0:T(8,128)(2,1)} %dd.1) | copy-start | bytes 1769476
  0.0 73.6 %copy-start.4 = (f32[4,6144]{1,0:T(4,128)S(1)}, f32[4,6144]{1,0:T(4,128)}, u32[]{:S(2)}) copy-start(f32[4,6144]{1,0:T(4,128)} %conv.1) | copy-start | bytes 294916
